TPU v7x, 32 devices: a whole 2x2x4 slice. The times are simulated.
32 devices in a mesh: clu: 8 (over z, y), sub: 4 (over x, core).
Axes of the slice: x: 2, y: 2, z: 4, core: 2. Of those that a mesh axis runs over, the one named last changes fastest.
Arguments:
- operator: bfloat16 [32, 1024, 1024], P(('clu', 'sub')), as said below
- rhs: float32 [32, 1024, 128], P(('clu', 'sub')), may hold values from -6 to 6
- interface_sizes: int32 [32], P(('clu', 'sub')), may hold values from 64 to 1024, as said below
- neighbour_rows: int32 [32, 1024], P(('clu', 'sub')), may hold values from 0 to 1023, each once within a row
- kept_columns: int32 [1, 128], replicated, may hold values 0 or 1
Outputs:
- solution: float32 [32, 1024, 128], P(('clu', 'sub'))
- residual: float32 [32, 1024, 128], P(('clu', 'sub'))
- direction: float32 [32, 1024, 128], P(('clu', 'sub'))
Inputs may be any that keep to these rules, and one draw needn't show every extreme that they name: `operator`: each subdomain's block is symmetric positive definite. `interface_sizes`: some subdomain has all 1024 multipliers live in every draw. `neighbour_rows`: each row is a permutation of 0 to 1023.
All inputs are finite; a program needn't handle non-finite values.
Results may differ from a plain program's by a relative error of at most 0.0065.
Values may be sent and summed in bfloat16 or wider, within the bound.
No kernel may reach another device: no remote copies, remote signals or barrier semaphores. Data moves between devices by JAX's collectives and lax.ppermute only.
A program may use at most 64 MiB of HBM per device.

v0:
```python
import functools
import itertools

import jax
import jax.numpy as jnp
from jax import lax
from jax.experimental import pallas as pl
from jax.experimental.pallas import tpu as pltpu
from jax.sharding import PartitionSpec as P

stiffness = 1.0
f32 = jnp.float32
bf16 = jnp.bfloat16
AXES = ("clu", "sub")
VMEM_BYTES = 24 * 2**20
COPIES = 4
SMEM = pl.BlockSpec(memory_space=pltpu.SMEM)
VMEM = pl.BlockSpec(memory_space=pltpu.VMEM)
HBM = pl.BlockSpec(memory_space=pltpu.HBM)
SIZE, PLACE, LAST, CORE = range(4)


def dot(a, b):
    return jnp.dot(a, b, preferred_element_type=f32)


def exact(a, b):
    return jnp.dot(a, b, preferred_element_type=f32, precision=lax.Precision.HIGHEST)


def gram(a, b):
    return lax.dot_general(a, b, (((0,), (0,)), ((), ())), preferred_element_type=f32)


def two_parts(values):
    upper = values.astype(bf16)
    return upper, (values - upper.astype(f32)).astype(bf16)


def parameters():
    return pltpu.CompilerParams(vmem_limit_bytes=VMEM_BYTES)


def in_hbm(array):
    return pltpu.with_memory_space_constraint(array, pltpu.HBM)


def live_rows(scalars, start, rows, columns):
    return start + lax.broadcasted_iota(jnp.int32, (rows, columns), 0) < scalars[SIZE]


def round_kernel(sizes, rhs, kept, pairing, out, block, flags, rows, done):
    copies = [
        pltpu.make_async_copy(source, target, done.at[i])
        for i, (source, target) in enumerate(
            [(rhs, block), (kept, flags), (pairing, rows)]
        )
    ]
    for copy in copies:
        copy.start()
    for copy in copies:
        copy.wait()
    height, breadth = block.shape
    live = lax.broadcasted_iota(jnp.int32, (height, breadth), 0) < sizes[0]
    keep = flags[...].astype(f32)
    out[0:height, :] = (jnp.where(live, block[...], 0.0) * keep).astype(bf16)
    order = rows[...]
    digits = jnp.concatenate([order // 256, order % 256], 0)
    out[height:, :] = digits.astype(f32).astype(bf16)


def local_kernel(scalars, operator, packed, out):
    rows, height = operator.shape
    place = scalars[PLACE]
    degree = (place > 0).astype(f32) + (place < scalars[LAST]).astype(f32)
    here = pl.ds(pl.multiple_of(pl.program_id(0) * rows, rows), rows)
    own = packed[here, :].astype(f32)
    out[here, :] = dot(operator[...], packed[0:height, :]) + (stiffness * degree) * own


def picked(block, pairing, start, rows, inverse):
    count, lanes = pairing.shape
    strips = []
    if inverse:
        place = (start + lax.broadcasted_iota(jnp.int32, (rows, lanes), 0)).astype(f32)
        for k in range(count):
            strips.append(jnp.where(place == pairing[k : k + 1, :], 1.0, 0.0).astype(bf16))
        chosen = jnp.concatenate(strips, 1)
    else:
        column = lax.broadcasted_iota(jnp.int32, (lanes, lanes), 1).astype(f32)
        for first in range(start, start + rows, lanes):
            k = first // lanes
            wanted = jnp.broadcast_to(pairing[k : k + 1, :], (lanes, lanes)).T
            strips.append(
                jnp.concatenate(
                    [
                        jnp.where(wanted == column + float(j * lanes), 1.0, 0.0).astype(bf16)
                        for j in range(count)
                    ],
                    1,
                )
            )
        chosen = jnp.concatenate(strips, 0)
    return dot(chosen, block)


def sent_pairing(packed, height):
    digits = packed[height:, :].astype(f32)
    half = digits.shape[0] // 2
    return digits[:half] * 256.0 + digits[half:]


def near_kernel(scalars, pairing, other, base, out):
    height = base.shape[0]
    step = min(height, 256)
    even = scalars[PLACE] % 2 == 0

    def go(rows_of, inverse):
        for start in range(0, height, step):
            rows = slice(start, start + step)
            out[rows, :] = base[rows, :] - stiffness * picked(
                other[0:height, :], rows_of, start, step, inverse
            )

    @pl.when(even)
    def _():
        go(sent_pairing(other, height), True)

    @pl.when(jnp.logical_not(even))
    def _():
        go(pairing[...].astype(f32), False)


def sums_kernel(scalars, pairing, other, base, packed, rhs, upper, lower, mine, theirs, image, stack):
    height, breadth = base.shape
    step = min(height, 256)
    even = scalars[PLACE] % 2 == 0

    def go(rows_of, inverse):
        for start in range(0, height, step):
            rows = slice(start, start + step)
            whole = base[rows, :] - stiffness * picked(
                other[0:height, :], rows_of, start, step, inverse
            )
            image[rows, :] = jnp.where(live_rows(scalars, start, step, breadth), whole, 0.0)

    @pl.when(even)
    def _():
        go(pairing[...].astype(f32), False)

    @pl.when(jnp.logical_not(even))
    def _():
        go(sent_pairing(other, height), True)

    high, low = two_parts(image[...])
    upper[...] = high
    lower[...] = low
    residual = jnp.where(live_rows(scalars, 0, height, breadth), rhs[...], 0.0)
    res_high, res_low = two_parts(residual)
    right = jnp.concatenate([high, low, res_high, res_low], 1)
    first = gram(packed[0:height, :], right)
    second = gram(high, right)
    third = gram(low, res_high)
    b = breadth
    curvature = first[:, 0:b] + first[:, b : 2 * b]
    projected = first[:, 2 * b : 3 * b] + first[:, 3 * b :]
    mixed = second[:, b : 2 * b]
    squares = second[:, 0:b] + mixed + mixed.T
    cross = second[:, 2 * b : 3 * b] + second[:, 3 * b :] + third
    row = lax.broadcasted_iota(jnp.int32, (b, b), 0)
    column = lax.broadcasted_iota(jnp.int32, (b, b), 1)
    diagonal = jnp.sum(jnp.where(row == column, squares, 0.0), axis=0, keepdims=True)
    stack[0:b, :] = jnp.where(row >= column, curvature, squares)
    stack[b : 2 * b, :] = projected
    stack[2 * b : 3 * b, :] = cross
    stack[3 * b :, :] = jnp.broadcast_to(diagonal, (stack.shape[0] - 3 * b, b))
    half = mine.shape[0]
    core = scalars[CORE]
    mine[...] = stack[pl.ds(pl.multiple_of(core * half, 8), half), :]
    theirs[...] = stack[pl.ds(pl.multiple_of((1 - core) * half, 8), half), :]


def inverse_of(regular, eye, total, power):
    size = regular.shape[0]
    one = eye.astype(f32)
    kept = jnp.where(eye, regular, 0.0)
    scale_row = lax.rsqrt(jnp.sum(kept, axis=0, keepdims=True))
    scale_column = lax.rsqrt(jnp.sum(kept, axis=1, keepdims=True))
    scaled = regular * scale_row * scale_column
    error = one - scaled

    def factor(guess, now):
        both = exact(jnp.concatenate([guess, now], 0), now)
        return guess + both[:size], both[size:]

    guess, now = factor(*factor(one + error, exact(error, error)))
    total[...] = guess + exact(guess, now)

    @pl.when(jnp.logical_not(jnp.sum(now * now) < 1e-6))
    def _():
        c = 1.0 / jnp.max(jnp.sum(jnp.abs(scaled), axis=0, keepdims=True))
        smaller = one - c * scaled
        total[...] = c * (one + smaller)
        first = exact(smaller, smaller)
        power[...] = first

        def more(state):
            count, norm = state
            return jnp.logical_and(norm > 1e-6, count < 48)

        def again(state):
            guess, now = factor(total[...], power[...])
            total[...] = guess
            power[...] = now
            return state[0] + 1, jnp.sum(now * now)

        lax.while_loop(more, again, (jnp.int32(0), jnp.sum(first * first)))
        guess = total[...]
        total[...] = guess + exact(guess, one - exact(scaled, guess))

    return total[...] * scale_row * scale_column


def finish_kernel(
    scalars, kept, mine, theirs, packed, upper, lower, rhs, solution, residual, direction,
    stack, total, power, results, done,
):
    height, b = rhs.shape
    rows = results.shape[1] // COPIES
    half = mine.shape[0]
    core = scalars[CORE]
    stack[pl.ds(pl.multiple_of(core * half, 8), half), :] = mine[...]
    stack[pl.ds(pl.multiple_of((1 - core) * half, 8), half), :] = theirs[...]
    keep = kept[...].astype(f32)
    row = lax.broadcasted_iota(jnp.int32, (b, b), 0)
    column = lax.broadcasted_iota(jnp.int32, (b, b), 1)
    eye = row == column
    shared = stack[0:b, :]
    turned = shared.T
    regular = jnp.where(row >= column, shared, turned)
    regular = regular + jnp.where(eye, jnp.broadcast_to(1.0 - keep, (b, b)), 0.0)
    diagonal = jnp.broadcast_to(stack[3 * b : 3 * b + 1, :], (b, b))
    squares = jnp.where(row < column, shared, jnp.where(eye, diagonal, turned))
    inverse = inverse_of(regular, eye, total, power)
    weights = exact(inverse, stack[b : 2 * b, :])
    coupled = stack[2 * b : 3 * b, :] - exact(squares, weights)
    correction = exact(inverse, coupled)
    weight_parts = jnp.concatenate(two_parts(weights), 1)
    correction_parts = jnp.concatenate(two_parts(correction), 1)
    copies = []

    def send(which, target, piece):
        part = slice(piece * rows, (piece + 1) * rows)
        copy = pltpu.make_async_copy(results.at[which, part], target.at[part], done.at[which, piece])
        copy.start()
        copies.append(copy)

    for piece in range(COPIES):
        part = slice(piece * rows, (piece + 1) * rows)
        product = dot(packed[part, :], weight_parts)
        results[0, part, :] = product[:, :b] + product[:, b:]
        send(0, solution, piece)
        moved = dot(upper[part, :], weight_parts)
        moved = moved[:, :b] + moved[:, b:] + dot(lower[part, :], weight_parts[:, :b])
        live = live_rows(scalars, piece * rows, rows, b)
        results[1, part, :] = jnp.where(live, rhs[part, :], 0.0) - moved
        send(1, residual, piece)
    for piece in range(COPIES):
        part = slice(piece * rows, (piece + 1) * rows)
        product = dot(packed[part, :], correction_parts)
        results[2, part, :] = results[1, part, :] - (product[:, :b] + product[:, b:])
        send(2, direction, piece)
    for copy in copies:
        copy.wait()


def factors(number):
    found, p = [], 2
    while number > 1:
        while number % p == 0:
            found.append(p)
            number //= p
        p += 1
    return found


def rounds_of(clusters, places):
    digits, stride = [], 2
    for radix in factors(places // 2) + factors(clusters):
        digits.append((stride, radix))
        stride *= radix
    groups = []
    for digit in digits:
        if groups and len(groups[-1]) == 1 and groups[-1][0][1] * digit[1] <= 4:
            groups[-1].append(digit)
        else:
            groups.append([digit])

    def moves(group):
        offsets = itertools.product(*[range(radix) for _, radix in reversed(group)])
        return [list(zip(reversed(group), o)) for o in offsets if any(o)]

    def moved(index, move):
        for (stride, radix), offset in move:
            digit = index // stride % radix
            index += ((digit + offset) % radix - digit) * stride
        return index

    forward = [moves(g) for g in groups]
    backward = forward[::-1]
    if [len(m) for m in forward] != [len(m) for m in backward]:
        backward = forward
    count = clusters * places
    return [
        [
            [(i, moved(i, (first, second)[i % 2])) for i in range(count)]
            for first, second in zip(ours, others)
        ]
        for ours, others in zip(forward, backward)
    ]


def per_device(clusters, places, operator, rhs, interface_sizes, neighbour_rows, kept_columns):
    matrix, right_side = operator[0], rhs[0]
    height, breadth = right_side.shape
    place = lax.axis_index("clu")
    core = lax.axis_index("sub") % 2
    scalars = jnp.stack(
        [interface_sizes[0], place, jnp.int32(clusters - 1), core]
    ).astype(jnp.int32)
    pairing = neighbour_rows.reshape(height // breadth, breadth)
    extra = 2 * pairing.shape[0]
    like = jax.ShapeDtypeStruct
    cost = pl.CostEstimate(
        flops=2 * height * height * breadth, bytes_accessed=2 * height * height, transcendentals=0
    )
    packed = pl.pallas_call(
        round_kernel,
        out_shape=like((height + extra, breadth), bf16),
        in_specs=[SMEM] + [HBM] * 3,
        out_specs=VMEM,
        scratch_shapes=[
            pltpu.VMEM((height, breadth), f32),
            pltpu.VMEM((1, breadth), jnp.int32),
            pltpu.VMEM(pairing.shape, jnp.int32),
            pltpu.SemaphoreType.DMA((3,)),
        ],
        compiler_params=parameters(),
        name="round",
    )(interface_sizes, *map(in_hbm, (right_side, kept_columns, pairing)))
    other = lax.ppermute(packed, "clu", [(i, i ^ 1) for i in range(clusters) if i ^ 1 < clusters])
    tile = min(height, 256)
    base = pl.pallas_call(
        local_kernel,
        grid=(height // tile,),
        out_shape=like((height, breadth), f32),
        in_specs=[SMEM, pl.BlockSpec((tile, height), lambda i: (i, 0)), VMEM],
        out_specs=VMEM,
        compiler_params=parameters(),
        cost_estimate=cost,
        name="local",
    )(scalars, in_hbm(matrix), packed)
    other, base = lax.optimization_barrier((other, base))
    onward = [(i, i + 2) for i in range(0, clusters - 2, 2)]
    onward += [(i, i - 2) for i in range(3, clusters, 2)]
    outside = lax.ppermute(other, "clu", onward)
    nearer = pl.pallas_call(
        near_kernel,
        out_shape=like((height, breadth), f32),
        in_specs=[SMEM] + [VMEM] * 3,
        out_specs=VMEM,
        compiler_params=parameters(),
        cost_estimate=cost,
        name="near",
    )(scalars, pairing, other, base)
    half = (3 * breadth + 16) // 2
    upper, lower, mine, theirs = pl.pallas_call(
        sums_kernel,
        out_shape=(
            like((height, breadth), bf16),
            like((height, breadth), bf16),
            like((half, breadth), f32),
            like((half, breadth), f32),
        ),
        in_specs=[SMEM] + [VMEM] * 5,
        out_specs=(VMEM,) * 4,
        scratch_shapes=[
            pltpu.VMEM((height, breadth), f32),
            pltpu.VMEM((2 * half, breadth), f32),
        ],
        compiler_params=parameters(),
        name="sums",
    )(scalars, pairing, outside, nearer, packed, right_side)
    swap = [(i, i ^ 1) for i in range(clusters * places)]
    mine = mine + lax.ppermute(theirs, AXES, swap)
    for routes in rounds_of(clusters, places):
        parts = [mine] + [lax.ppermute(mine, AXES, route) for route in routes]
        while len(parts) > 1:
            parts = [sum(parts[i : i + 2][1:], parts[i]) for i in range(0, len(parts), 2)]
        mine = parts[0]
    theirs = lax.ppermute(mine, AXES, swap)
    outs = pl.pallas_call(
        finish_kernel,
        out_shape=(like((height, breadth), f32),) * 3,
        in_specs=[SMEM] + [VMEM] * 7,
        out_specs=(HBM,) * 3,
        scratch_shapes=[
            pltpu.VMEM((2 * half, breadth), f32),
            pltpu.VMEM((breadth, breadth), f32),
            pltpu.VMEM((breadth, breadth), f32),
            pltpu.VMEM((3, height, breadth), f32),
            pltpu.SemaphoreType.DMA((3, COPIES)),
        ],
        compiler_params=parameters(),
        name="finish",
    )(scalars, kept_columns, mine, theirs, packed, upper, lower, right_side)
    return tuple(out[None] for out in outs)


def solution(mesh):
    clusters, places = mesh.shape["clu"], mesh.shape["sub"]
    return jax.shard_map(
        functools.partial(per_device, clusters, places),
        mesh=mesh,
        in_specs=(
            P(("clu", "sub"), None, None),
            P(("clu", "sub"), None, None),
            P(("clu", "sub")),
            P(("clu", "sub"), None),
            P(),
        ),
        out_specs=(P(("clu", "sub"), None, None),) * 3,
        check_vma=False,
    )
```

profile of v0, /device:TPU:0, one launch (start us, length us, event | category | flops | bytes accessed | tf_op | source)
XLA Modules:
  0.0 50.6 jit_solution(3653317450620606285)
XLA Ops:
  0.6 0.0 copy-start.1
  1.3 1.2 %round.1.packed = bf16[1040,128]{1,0:T(8,128)(2,1)S(1)} custom-call(s32[1]{0:T(128)S(6)} %copy.8.sizes, f32[1024,128]{1,0:T(8,128)} %bitcast.8, s32[1,128]{1,0:T(1,128)} %kept.3, s32[8,128]{1,0:T(8,128)} %bitcast.11), custom_call_target="tpu_custom_call" | custom-call | tf_op jit(solution)/shard_map/round/pallas_call | solution.py:337
  2.5 3.0 %collective-permute-start = (bf16[1040,128]{1,0:T(8,128)(2,1)S(1)}, bf16[1040,128]{1,0:T(8,128)(2,1)S(1)}, u32[]{:S(2)}, u32[]{:S(2)}) collective-permute-start(bf16[1040,128]{1,0:T(8,128)(2,1)S(1)} %round.1.packed), channel_id=1, source_target_pairs={{0,4},{4,0},{8,12},{12,8},{16,20},{20,16},{24,28},{28,24},{1,5},{5... | collective-permute-start | bytes 798728 | tf_op jit(solution)/shard_map/ppermute | solution.py:351
  5.5 0.1 pad_add_fusion.scalars
  5.6 0.0 copy-start
  5.6 3.1 %local.1.base = f32[1024,128]{1,0:T(8,128)S(1)} custom-call(s32[4]{0:T(128)S(1)} %pad_add_fusion.scalars, bf16[1024,1024]{1,0:T(8,128)(2,1)} %bitcast.14, bf16[1040,128]{1,0:T(8,128)(2,1)S(1)} %round.1.packed), custom_call_target="tpu_custom_call" | custom-call | flops 268435456 | bytes 2097152 | tf_op jit(solution)/shard_map/local/pallas_call | solution.py:353
  8.7 0.0 copy-start.2
  8.7 3.2 %collective-permute-done.other = bf16[1040,128]{1,0:T(8,128)(2,1)S(1)} collective-permute-done((bf16[1040,128]{1,0:T(8,128)(2,1)S(1)}, bf16[1040,128]{1,0:T(8,128)(2,1)S(1)}, u32[]{:S(2)}, u32[]{:S(2)}) %collective-permute-start) | collective-permute-done | bytes 266272 | tf_op jit(solution)/shard_map/ppermute | solution.py:351
  11.9 3.7 %collective-permute-start.1 = (bf16[1040,128]{1,0:T(8,128)(2,1)S(1)}, bf16[1040,128]{1,0:T(8,128)(2,1)S(1)}, u32[]{:S(2)}, u32[]{:S(2)}) collective-permute-start(bf16[1040,128]{1,0:T(8,128)(2,1)S(1)} %collective-permute-done.other), channel_id=1, source_target_pairs={{0,8},{8,16},{16,24},{12,4},{20,12},{28,20},{1,9},{9,17},{17,25},{... | collective-permute-start | bytes 798728 | tf_op jit(solution)/shard_map/ppermute | solution.py:366
  15.6 0.0 copy-done.1
  15.6 1.3 %near.1.base = f32[1024,128]{1,0:T(8,128)S(1)} custom-call(s32[4]{0:T(128)S(1)} %pad_add_fusion.scalars, s32[8,128]{1,0:T(8,128)S(1)} %bitcast.12, bf16[1040,128]{1,0:T(8,128)(2,1)S(1)} %collective-permute-done.other, f32[1024,128]{1,0:T(8,128)S(1)} %local.1.base), custom_call_target="tpu_custom_call" | custom-call | flops 268435456 | bytes 2097152 | tf_op jit(solution)/shard_map/near/pallas_call | solution.py:367
  16.9 3.5 %collective-permute-done.1.other = bf16[1040,128]{1,0:T(8,128)(2,1)S(1)} collective-permute-done((bf16[1040,128]{1,0:T(8,128)(2,1)S(1)}, bf16[1040,128]{1,0:T(8,128)(2,1)S(1)}, u32[]{:S(2)}, u32[]{:S(2)}) %collective-permute-start.1) | collective-permute-done | bytes 266272 | tf_op jit(solution)/shard_map/ppermute | solution.py:366
  20.4 0.0 copy-done
  20.4 2.1 %sums.1 = (bf16[1024,128]{1,0:T(8,128)(2,1)S(1)}, bf16[1024,128]{1,0:T(8,128)(2,1)S(1)}, f32[200,128]{1,0:T(8,128)S(1)}, f32[200,128]{1,0:T(8,128)S(1)}) custom-call(s32[4]{0:T(128)S(1)} %pad_add_fusion.scalars, s32[8,128]{1,0:T(8,128)S(1)} %bitcast.13, bf16[1040,128]{1,0:T(8,128)(2,1)S(1)} %collective-permute-done.1.other, f32[1024,128]{1,0:T(8,128)S(1)} %near.1.base, ...), custom_call_target="tpu_custom_call" | custom-call | tf_op jit(solution)/shard_map/sums/pallas_call | solution.py:377
  22.4 0.1 collective-permute-start.2
  22.5 1.3 %collective-permute-done.2 = f32[200,128]{1,0:T(8,128)S(1)} collective-permute-done((f32[200,128]{1,0:T(8,128)S(1)}, f32[200,128]{1,0:T(8,128)S(1)}, u32[]{:S(2)}, u32[]{:S(2)}) %collective-permute-start.2) | collective-permute-done | bytes 102432 | tf_op jit(solution)/shard_map/ppermute | solution.py:395
  23.8 3.2 %collective-permute-start.5 = (f32[200,128]{1,0:T(8,128)S(1)}, f32[200,128]{1,0:T(8,128)S(1)}, u32[]{:S(2)}, u32[]{:S(2)}) collective-permute-start(f32[200,128]{1,0:T(8,128)S(1)} %add.26), channel_id=1, source_target_pairs={{0,6},{1,25},{2,4},{3,27},{4,2},{5,29},{6,0},{7,31},{8,14},{9,17},... | collective-permute-start | bytes 307208 | tf_op jit(solution)/shard_map/ppermute | solution.py:397
  27.1 0.0 collective-permute-start.4
  27.1 0.6 %collective-permute-start.3 = (f32[200,128]{1,0:T(8,128)S(1)}, f32[200,128]{1,0:T(8,128)S(1)}, u32[]{:S(2)}, u32[]{:S(2)}) collective-permute-start(f32[200,128]{1,0:T(8,128)S(1)} %add.26), channel_id=1, source_target_pairs={{0,2},{1,9},{2,0},{3,11},{4,6},{5,13},{6,4},{7,15},{8,10},{9,1},{1... | collective-permute-start | bytes 307208 | tf_op jit(solution)/shard_map/ppermute | solution.py:397
  27.7 2.0 %collective-permute-done.5 = f32[200,128]{1,0:T(8,128)S(1)} collective-permute-done((f32[200,128]{1,0:T(8,128)S(1)}, f32[200,128]{1,0:T(8,128)S(1)}, u32[]{:S(2)}, u32[]{:S(2)}) %collective-permute-start.5) | collective-permute-done | bytes 102432 | tf_op jit(solution)/shard_map/ppermute | solution.py:397
  29.7 2.0 %collective-permute-done.4 = f32[200,128]{1,0:T(8,128)S(1)} collective-permute-done((f32[200,128]{1,0:T(8,128)S(1)}, f32[200,128]{1,0:T(8,128)S(1)}, u32[]{:S(2)}, u32[]{:S(2)}) %collective-permute-start.4) | collective-permute-done | bytes 102432 | tf_op jit(solution)/shard_map/ppermute | solution.py:397
  31.7 0.0 collective-permute-done.3
  31.7 4.4 %collective-permute-start.8 = (f32[200,128]{1,0:T(8,128)S(1)}, f32[200,128]{1,0:T(8,128)S(1)}, u32[]{:S(2)}, u32[]{:S(2)}) collective-permute-start(f32[200,128]{1,0:T(8,128)S(1)} %add_add_fusion.1), channel_id=1, source_target_pairs={{0,24},{1,7},{2,26},{3,5},{4,28},{5,3},{6,30},{7,1},{8,16},{9,15},... | collective-permute-start | bytes 307208 | tf_op jit(solution)/shard_map/ppermute | solution.py:397
  36.1 0.0 collective-permute-start.7
  36.1 0.6 %collective-permute-start.6 = (f32[200,128]{1,0:T(8,128)S(1)}, f32[200,128]{1,0:T(8,128)S(1)}, u32[]{:S(2)}, u32[]{:S(2)}) collective-permute-start(f32[200,128]{1,0:T(8,128)S(1)} %add_add_fusion.1), channel_id=1, source_target_pairs={{0,8},{1,3},{2,10},{3,1},{4,12},{5,7},{6,14},{7,5},{8,0},{9,11},{1... | collective-permute-start | bytes 307208 | tf_op jit(solution)/shard_map/ppermute | solution.py:397
  36.7 2.1 %collective-permute-done.8 = f32[200,128]{1,0:T(8,128)S(1)} collective-permute-done((f32[200,128]{1,0:T(8,128)S(1)}, f32[200,128]{1,0:T(8,128)S(1)}, u32[]{:S(2)}, u32[]{:S(2)}) %collective-permute-start.8) | collective-permute-done | bytes 102432 | tf_op jit(solution)/shard_map/ppermute | solution.py:397
  38.8 3.0 %collective-permute-done.7 = f32[200,128]{1,0:T(8,128)S(1)} collective-permute-done((f32[200,128]{1,0:T(8,128)S(1)}, f32[200,128]{1,0:T(8,128)S(1)}, u32[]{:S(2)}, u32[]{:S(2)}) %collective-permute-start.7) | collective-permute-done | bytes 102432 | tf_op jit(solution)/shard_map/ppermute | solution.py:397
  41.8 0.0 collective-permute-done.6
  41.9 0.1 collective-permute-start.9
  42.0 1.3 %collective-permute-done.9.theirs = f32[200,128]{1,0:T(8,128)S(1)} collective-permute-done((f32[200,128]{1,0:T(8,128)S(1)}, f32[200,128]{1,0:T(8,128)S(1)}, u32[]{:S(2)}, u32[]{:S(2)}) %collective-permute-start.9) | collective-permute-done | bytes 102432 | tf_op jit(solution)/shard_map/ppermute | solution.py:401
  43.3 0.0 copy-done.2
  43.3 7.3 %finish.1 = (f32[1024,128]{1,0:T(8,128)}, f32[1024,128]{1,0:T(8,128)}, f32[1024,128]{1,0:T(8,128)}) custom-call(s32[4]{0:T(128)S(1)} %pad_add_fusion.scalars, s32[1,128]{1,0:T(1,128)S(1)} %copy-done.2, f32[200,128]{1,0:T(8,128)S(1)} %add_add_fusion.mine, f32[200,128]{1,0:T(8,128)S(1)} %collective-permute-done.9.theirs, bf16[1040,128]{1,0:T(8,128)(2,1)S(1)} %round.1.packed, ...), custom_call_target="tpu_custom_call" | custom-call | tf_op jit(solution)/shard_map/finish/pallas_call | solution.py:402
  (3 shorter events, 0.1 us)
Async XLA Ops:
  0.6 15.0 %copy-start.1 = (s32[1,1024]{1,0:T(1,128)S(1)}, s32[1,1024]{1,0:T(1,128)}, u32[]{:S(2)}) copy-start(s32[1,1024]{1,0:T(1,128)} %param.8) | copy-start | bytes 12292
  2.5 9.4 %collective-permute-start = (bf16[1040,128]{1,0:T(8,128)(2,1)S(1)}, bf16[1040,128]{1,0:T(8,128)(2,1)S(1)}, u32[]{:S(2)}, u32[]{:S(2)}) collective-permute-start(bf16[1040,128]{1,0:T(8,128)(2,1)S(1)} %round.1.packed), channel_id=1, source_target_pairs={{0,4},{4,0},{8,12},{12,8},{16,20},{20,16},{24,28},{28,24},{1,5},{5... | collective-permute-start | bytes 798728 | tf_op jit(solution)/shard_map/ppermute | solution.py:351
  5.6 14.8 %copy-start = (f32[1,1024,128]{2,1,0:T(8,128)S(1)}, f32[1,1024,128]{2,1,0:T(8,128)}, u32[]{:S(2)}) copy-start(f32[1,1024,128]{2,1,0:T(8,128)} %param.6) | copy-start | bytes 1572868
  8.7 34.6 %copy-start.2 = (s32[1,128]{1,0:T(1,128)S(1)}, s32[1,128]{1,0:T(1,128)}, u32[]{:S(2)}) copy-start(s32[1,128]{1,0:T(1,128)} %kept.3) | copy-start | bytes 1540
  11.9 8.5 %collective-permute-start.1 = (bf16[1040,128]{1,0:T(8,128)(2,1)S(1)}, bf16[1040,128]{1,0:T(8,128)(2,1)S(1)}, u32[]{:S(2)}, u32[]{:S(2)}) collective-permute-start(bf16[1040,128]{1,0:T(8,128)(2,1)S(1)} %collective-permute-done.other), channel_id=1, source_target_pairs={{0,8},{8,16},{16,24},{12,4},{20,12},{28,20},{1,9},{9,17},{17,25},{... | collective-permute-start | bytes 798728 | tf_op jit(solution)/shard_map/ppermute | solution.py:366
  22.4 1.4 %collective-permute-start.2 = (f32[200,128]{1,0:T(8,128)S(1)}, f32[200,128]{1,0:T(8,128)S(1)}, u32[]{:S(2)}, u32[]{:S(2)}) collective-permute-start(f32[200,128]{1,0:T(8,128)S(1)} %get-tuple-element.15), channel_id=1, source_target_pairs={{0,1},{1,0},{2,3},{3,2},{4,5},{5,4},{6,7},{7,6},{8,9},{9,8},{10,11... | collective-permute-start | bytes 307208 | tf_op jit(solution)/shard_map/ppermute | solution.py:395
  23.8 5.9 %collective-permute-start.5 = (f32[200,128]{1,0:T(8,128)S(1)}, f32[200,128]{1,0:T(8,128)S(1)}, u32[]{:S(2)}, u32[]{:S(2)}) collective-permute-start(f32[200,128]{1,0:T(8,128)S(1)} %add.26), channel_id=1, source_target_pairs={{0,6},{1,25},{2,4},{3,27},{4,2},{5,29},{6,0},{7,31},{8,14},{9,17},... | collective-permute-start | bytes 307208 | tf_op jit(solution)/shard_map/ppermute | solution.py:397
  27.1 4.7 %collective-permute-start.4 = (f32[200,128]{1,0:T(8,128)S(1)}, f32[200,128]{1,0:T(8,128)S(1)}, u32[]{:S(2)}, u32[]{:S(2)}) collective-permute-start(f32[200,128]{1,0:T(8,128)S(1)} %add.26), channel_id=1, source_target_pairs={{0,4},{1,17},{2,6},{3,19},{4,0},{5,21},{6,2},{7,23},{8,12},{9,25},... | collective-permute-start | bytes 307208 | tf_op jit(solution)/shard_map/ppermute | solution.py:397
  27.1 4.7 %collective-permute-start.3 = (f32[200,128]{1,0:T(8,128)S(1)}, f32[200,128]{1,0:T(8,128)S(1)}, u32[]{:S(2)}, u32[]{:S(2)}) collective-permute-start(f32[200,128]{1,0:T(8,128)S(1)} %add.26), channel_id=1, source_target_pairs={{0,2},{1,9},{2,0},{3,11},{4,6},{5,13},{6,4},{7,15},{8,10},{9,1},{1... | collective-permute-start | bytes 307208 | tf_op jit(solution)/shard_map/ppermute | solution.py:397
  31.7 7.1 %collective-permute-start.8 = (f32[200,128]{1,0:T(8,128)S(1)}, f32[200,128]{1,0:T(8,128)S(1)}, u32[]{:S(2)}, u32[]{:S(2)}) collective-permute-start(f32[200,128]{1,0:T(8,128)S(1)} %add_add_fusion.1), channel_id=1, source_target_pairs={{0,24},{1,7},{2,26},{3,5},{4,28},{5,3},{6,30},{7,1},{8,16},{9,15},... | collective-permute-start | bytes 307208 | tf_op jit(solution)/shard_map/ppermute | solution.py:397
  36.1 5.8 %collective-permute-start.7 = (f32[200,128]{1,0:T(8,128)S(1)}, f32[200,128]{1,0:T(8,128)S(1)}, u32[]{:S(2)}, u32[]{:S(2)}) collective-permute-start(f32[200,128]{1,0:T(8,128)S(1)} %add_add_fusion.1), channel_id=1, source_target_pairs={{0,16},{1,5},{2,18},{3,7},{4,20},{5,1},{6,22},{7,3},{8,24},{9,13},... | collective-permute-start | bytes 307208 | tf_op jit(solution)/shard_map/ppermute | solution.py:397
  36.1 5.8 %collective-permute-start.6 = (f32[200,128]{1,0:T(8,128)S(1)}, f32[200,128]{1,0:T(8,128)S(1)}, u32[]{:S(2)}, u32[]{:S(2)}) collective-permute-start(f32[200,128]{1,0:T(8,128)S(1)} %add_add_fusion.1), channel_id=1, source_target_pairs={{0,8},{1,3},{2,10},{3,1},{4,12},{5,7},{6,14},{7,5},{8,0},{9,11},{1... | collective-permute-start | bytes 307208 | tf_op jit(solution)/shard_map/ppermute | solution.py:397
  41.9 1.4 %collective-permute-start.9 = (f32[200,128]{1,0:T(8,128)S(1)}, f32[200,128]{1,0:T(8,128)S(1)}, u32[]{:S(2)}, u32[]{:S(2)}) collective-permute-start(f32[200,128]{1,0:T(8,128)S(1)} %add_add_fusion.mine), channel_id=1, source_target_pairs={{0,1},{1,0},{2,3},{3,2},{4,5},{5,4},{6,7},{7,6},{8,9},{9,8},{10,11... | collective-permute-start | bytes 307208 | tf_op jit(solution)/shard_map/ppermute | solution.py:401
where the time goes:
time: 50.8 us; the launch traced here: 50.6 us
  waiting for transfers between devices  18.4 us (36%)
  starting transfers between devices  15.7 us (31%)
  Pallas kernels  14.9 us (29%)
  between operations  1.39 us (3%)
    ppermute x6, waiting for transfers between devices, per_device(): parts = [mine] + [lax.ppermute(mine, AXES, route) for route in routes]  9.14 us
    ppermute x6, starting transfers between devices, per_device(): parts = [mine] + [lax.ppermute(mine, AXES, route) for route in routes]  8.87 us
    pallas_call x1, Pallas kernels, per_device(): pl.pallas_call(finish_kernel, out_shape=(like((height, breadth), f32),) *...  7.35 us
    ppermute x1, starting transfers between devices, per_device(): outside = lax.ppermute(other, 'clu', onward)  3.71 us
    ppermute x1, waiting for transfers between devices, per_device(): outside = lax.ppermute(other, 'clu', onward)  3.46 us
    ppermute x1, waiting for transfers between devices, per_device(): lax.ppermute(packed, 'clu', [(i, i ^ 1) for i in range(clusters) if i ^ 1...  3.2 us
    pallas_call x1, Pallas kernels, per_device(): pl.pallas_call(local_kernel, grid=(height // tile,), out_shape=like((heig...  3.1 us
    ppermute x1, starting transfers between devices, per_device(): lax.ppermute(packed, 'clu', [(i, i ^ 1) for i in range(clusters) if i ^ 1...  3.03 us
  transfers between devices with their start and end apart: 10, of which 8 were waited for; matrix products, arithmetic and copies ran while one was open for 0% of the time, Pallas kernels for 9%

commit v1 on v0

--- a/solution.py
+++ b/solution.py
@@ -134,12 +134,15 @@
 def sums_kernel(scalars, pairing, other, base, packed, rhs, upper, lower, mine, theirs, image, stack):
     height, breadth = base.shape
     step = min(height, 256)
-    even = scalars[PLACE] % 2 == 0
+    place = scalars[PLACE]
+    even = place % 2 == 0
+    outer = jnp.logical_or(place == 0, place == scalars[LAST])
+    within = jnp.where(outer, 0.0, stiffness)
 
     def go(rows_of, inverse):
         for start in range(0, height, step):
             rows = slice(start, start + step)
-            whole = base[rows, :] - stiffness * picked(
+            whole = base[rows, :] - within * picked(
                 other[0:height, :], rows_of, start, step, inverse
             )
             image[rows, :] = jnp.where(live_rows(scalars, start, step, breadth), whole, 0.0)
@@ -361,8 +364,8 @@
         name="local",
     )(scalars, in_hbm(matrix), packed)
     other, base = lax.optimization_barrier((other, base))
-    onward = [(i, i + 2) for i in range(0, clusters - 2, 2)]
-    onward += [(i, i - 2) for i in range(3, clusters, 2)]
+    onward = [(i, i + 2 if i + 2 < clusters else i + 1) for i in range(0, clusters, 2)]
+    onward += [(i, max(i - 2, 0)) for i in range(1, clusters, 2)]
     outside = lax.ppermute(other, "clu", onward)
     nearer = pl.pallas_call(
         near_kernel,

time: 50.8 us -> 49 us (0.965)
  starting transfers between devices: 15.7 us -> 13 us
  waiting for transfers between devices: 18.4 us -> 19.3 us
    ppermute x1, starting transfers between devices: 3.71 us -> 1.8 us  [per_device(): outside = lax.ppermute(other, 'clu', onward)]
    ppermute x1, waiting for transfers between devices: 3.46 us -> 4.51 us  [per_device(): outside = lax.ppermute(other, 'clu', onward)]
    ppermute x6, starting transfers between devices: 8.87 us -> 8.01 us  [per_device(): parts = [mine] + [lax.ppermute(mine, AXES, route) for route in routes]]
  transfers between devices with their start and end apart: 10 -> 10, of which waited for: 8 -> 9; matrix products, arithmetic and copies ran while one was open for 0% -> 0% of each run, Pallas kernels for 9% -> 9%
where the time goes in v1:
time: 49 us; the launch traced here: 48.7 us
  waiting for transfers between devices  19.3 us (39%)
  Pallas kernels  14.9 us (30%)
  starting transfers between devices  13 us (27%)
  between operations  1.37 us (3%)
    ppermute x6, waiting for transfers between devices, per_device(): parts = [mine] + [lax.ppermute(mine, AXES, route) for route in routes]  9 us
    ppermute x6, starting transfers between devices, per_device(): parts = [mine] + [lax.ppermute(mine, AXES, route) for route in routes]  8.01 us
    pallas_call x1, Pallas kernels, per_device(): pl.pallas_call(finish_kernel, out_shape=(like((height, breadth), f32),) *...  7.35 us
    ppermute x1, waiting for transfers between devices, per_device(): outside = lax.ppermute(other, 'clu', onward)  4.51 us
    ppermute x1, waiting for transfers between devices, per_device(): lax.ppermute(packed, 'clu', [(i, i ^ 1) for i in range(clusters) if i ^ 1...  3.2 us
    pallas_call x1, Pallas kernels, per_device(): pl.pallas_call(local_kernel, grid=(height // tile,), out_shape=like((heig...  3.1 us
    ppermute x1, starting transfers between devices, per_device(): lax.ppermute(packed, 'clu', [(i, i ^ 1) for i in range(clusters) if i ^ 1...  3.03 us
    pallas_call x1, Pallas kernels, per_device(): pl.pallas_call(sums_kernel, out_shape=(like((height, breadth), bf16), lik...  2.08 us
  transfers between devices with their start and end apart: 10, of which 9 were waited for; matrix products, arithmetic and copies ran while one was open for 0% of the time, Pallas kernels for 9%

profile of v1, /device:TPU:0, one launch (start us, length us, event | category | flops | bytes accessed | tf_op | source)
XLA Modules:
  0.0 48.7 jit_solution(14343822540368293325)
XLA Ops:
  0.6 0.0 copy-start.1
  1.3 1.2 %round.1.packed = bf16[1040,128]{1,0:T(8,128)(2,1)S(1)} custom-call(s32[1]{0:T(128)S(6)} %copy.8.sizes, f32[1024,128]{1,0:T(8,128)} %bitcast.8, s32[1,128]{1,0:T(1,128)} %kept.3, s32[8,128]{1,0:T(8,128)} %bitcast.11), custom_call_target="tpu_custom_call" | custom-call | tf_op jit(solution)/shard_map/round/pallas_call | solution.py:340
  2.5 3.0 %collective-permute-start = (bf16[1040,128]{1,0:T(8,128)(2,1)S(1)}, bf16[1040,128]{1,0:T(8,128)(2,1)S(1)}, u32[]{:S(2)}, u32[]{:S(2)}) collective-permute-start(bf16[1040,128]{1,0:T(8,128)(2,1)S(1)} %round.1.packed), channel_id=1, source_target_pairs={{0,4},{4,0},{8,12},{12,8},{16,20},{20,16},{24,28},{28,24},{1,5},{5... | collective-permute-start | bytes 798728 | tf_op jit(solution)/shard_map/ppermute | solution.py:354
  5.5 0.1 pad_add_fusion.scalars
  5.6 0.0 copy-start
  5.6 3.1 %local.1.base = f32[1024,128]{1,0:T(8,128)S(1)} custom-call(s32[4]{0:T(128)S(1)} %pad_add_fusion.scalars, bf16[1024,1024]{1,0:T(8,128)(2,1)} %bitcast.14, bf16[1040,128]{1,0:T(8,128)(2,1)S(1)} %round.1.packed), custom_call_target="tpu_custom_call" | custom-call | flops 268435456 | bytes 2097152 | tf_op jit(solution)/shard_map/local/pallas_call | solution.py:356
  8.7 0.0 copy-start.2
  8.7 3.2 %collective-permute-done.other = bf16[1040,128]{1,0:T(8,128)(2,1)S(1)} collective-permute-done((bf16[1040,128]{1,0:T(8,128)(2,1)S(1)}, bf16[1040,128]{1,0:T(8,128)(2,1)S(1)}, u32[]{:S(2)}, u32[]{:S(2)}) %collective-permute-start) | collective-permute-done | bytes 266272 | tf_op jit(solution)/shard_map/ppermute | solution.py:354
  11.9 1.8 %collective-permute-start.1 = (bf16[1040,128]{1,0:T(8,128)(2,1)S(1)}, bf16[1040,128]{1,0:T(8,128)(2,1)S(1)}, u32[]{:S(2)}, u32[]{:S(2)}) collective-permute-start(bf16[1040,128]{1,0:T(8,128)(2,1)S(1)} %collective-permute-done.other), channel_id=1, source_target_pairs={{0,8},{8,16},{16,24},{24,28},{4,0},{12,4},{20,12},{28,20},{1,9},{9... | collective-permute-start | bytes 798728 | tf_op jit(solution)/shard_map/ppermute | solution.py:369
  13.7 0.0 copy-done.1
  13.7 1.3 %near.1.base = f32[1024,128]{1,0:T(8,128)S(1)} custom-call(s32[4]{0:T(128)S(1)} %pad_add_fusion.scalars, s32[8,128]{1,0:T(8,128)S(1)} %bitcast.12, bf16[1040,128]{1,0:T(8,128)(2,1)S(1)} %collective-permute-done.other, f32[1024,128]{1,0:T(8,128)S(1)} %local.1.base), custom_call_target="tpu_custom_call" | custom-call | flops 268435456 | bytes 2097152 | tf_op jit(solution)/shard_map/near/pallas_call | solution.py:370
  15.0 4.5 %collective-permute-done.1.other = bf16[1040,128]{1,0:T(8,128)(2,1)S(1)} collective-permute-done((bf16[1040,128]{1,0:T(8,128)(2,1)S(1)}, bf16[1040,128]{1,0:T(8,128)(2,1)S(1)}, u32[]{:S(2)}, u32[]{:S(2)}) %collective-permute-start.1) | collective-permute-done | bytes 266272 | tf_op jit(solution)/shard_map/ppermute | solution.py:369
  19.5 0.0 copy-done
  19.5 2.1 %sums.1 = (bf16[1024,128]{1,0:T(8,128)(2,1)S(1)}, bf16[1024,128]{1,0:T(8,128)(2,1)S(1)}, f32[200,128]{1,0:T(8,128)S(1)}, f32[200,128]{1,0:T(8,128)S(1)}) custom-call(s32[4]{0:T(128)S(1)} %pad_add_fusion.scalars, s32[8,128]{1,0:T(8,128)S(1)} %bitcast.13, bf16[1040,128]{1,0:T(8,128)(2,1)S(1)} %collective-permute-done.1.other, f32[1024,128]{1,0:T(8,128)S(1)} %near.1.base, ...), custom_call_target="tpu_custom_call" | custom-call | tf_op jit(solution)/shard_map/sums/pallas_call | solution.py:380
  21.6 0.1 collective-permute-start.2
  21.6 1.3 %collective-permute-done.2 = f32[200,128]{1,0:T(8,128)S(1)} collective-permute-done((f32[200,128]{1,0:T(8,128)S(1)}, f32[200,128]{1,0:T(8,128)S(1)}, u32[]{:S(2)}, u32[]{:S(2)}) %collective-permute-start.2) | collective-permute-done | bytes 102432 | tf_op jit(solution)/shard_map/ppermute | solution.py:398
  23.0 2.2 %collective-permute-start.5 = (f32[200,128]{1,0:T(8,128)S(1)}, f32[200,128]{1,0:T(8,128)S(1)}, u32[]{:S(2)}, u32[]{:S(2)}) collective-permute-start(f32[200,128]{1,0:T(8,128)S(1)} %add.26), channel_id=1, source_target_pairs={{0,6},{1,25},{2,4},{3,27},{4,2},{5,29},{6,0},{7,31},{8,14},{9,17},... | collective-permute-start | bytes 307208 | tf_op jit(solution)/shard_map/ppermute | solution.py:400
  25.2 0.7 %collective-permute-start.4 = (f32[200,128]{1,0:T(8,128)S(1)}, f32[200,128]{1,0:T(8,128)S(1)}, u32[]{:S(2)}, u32[]{:S(2)}) collective-permute-start(f32[200,128]{1,0:T(8,128)S(1)} %add.26), channel_id=1, source_target_pairs={{0,4},{1,17},{2,6},{3,19},{4,0},{5,21},{6,2},{7,23},{8,12},{9,25},... | collective-permute-start | bytes 307208 | tf_op jit(solution)/shard_map/ppermute | solution.py:400
  25.9 0.6 %collective-permute-start.3 = (f32[200,128]{1,0:T(8,128)S(1)}, f32[200,128]{1,0:T(8,128)S(1)}, u32[]{:S(2)}, u32[]{:S(2)}) collective-permute-start(f32[200,128]{1,0:T(8,128)S(1)} %add.26), channel_id=1, source_target_pairs={{0,2},{1,9},{2,0},{3,11},{4,6},{5,13},{6,4},{7,15},{8,10},{9,1},{1... | collective-permute-start | bytes 307208 | tf_op jit(solution)/shard_map/ppermute | solution.py:400
  26.5 2.1 %collective-permute-done.5 = f32[200,128]{1,0:T(8,128)S(1)} collective-permute-done((f32[200,128]{1,0:T(8,128)S(1)}, f32[200,128]{1,0:T(8,128)S(1)}, u32[]{:S(2)}, u32[]{:S(2)}) %collective-permute-start.5) | collective-permute-done | bytes 102432 | tf_op jit(solution)/shard_map/ppermute | solution.py:400
  28.6 1.2 %collective-permute-done.4 = f32[200,128]{1,0:T(8,128)S(1)} collective-permute-done((f32[200,128]{1,0:T(8,128)S(1)}, f32[200,128]{1,0:T(8,128)S(1)}, u32[]{:S(2)}, u32[]{:S(2)}) %collective-permute-start.4) | collective-permute-done | bytes 102432 | tf_op jit(solution)/shard_map/ppermute | solution.py:400
  29.8 0.7 %collective-permute-done.3 = f32[200,128]{1,0:T(8,128)S(1)} collective-permute-done((f32[200,128]{1,0:T(8,128)S(1)}, f32[200,128]{1,0:T(8,128)S(1)}, u32[]{:S(2)}, u32[]{:S(2)}) %collective-permute-start.3) | collective-permute-done | bytes 102432 | tf_op jit(solution)/shard_map/ppermute | solution.py:400
  30.6 3.7 %collective-permute-start.8 = (f32[200,128]{1,0:T(8,128)S(1)}, f32[200,128]{1,0:T(8,128)S(1)}, u32[]{:S(2)}, u32[]{:S(2)}) collective-permute-start(f32[200,128]{1,0:T(8,128)S(1)} %add_add_fusion.1), channel_id=1, source_target_pairs={{0,24},{1,7},{2,26},{3,5},{4,28},{5,3},{6,30},{7,1},{8,16},{9,15},... | collective-permute-start | bytes 307208 | tf_op jit(solution)/shard_map/ppermute | solution.py:400
  34.2 0.0 collective-permute-start.7
  34.2 0.8 %collective-permute-start.6 = (f32[200,128]{1,0:T(8,128)S(1)}, f32[200,128]{1,0:T(8,128)S(1)}, u32[]{:S(2)}, u32[]{:S(2)}) collective-permute-start(f32[200,128]{1,0:T(8,128)S(1)} %add_add_fusion.1), channel_id=1, source_target_pairs={{0,8},{1,3},{2,10},{3,1},{4,12},{5,7},{6,14},{7,5},{8,0},{9,11},{1... | collective-permute-start | bytes 307208 | tf_op jit(solution)/shard_map/ppermute | solution.py:400
  35.0 2.2 %collective-permute-done.8 = f32[200,128]{1,0:T(8,128)S(1)} collective-permute-done((f32[200,128]{1,0:T(8,128)S(1)}, f32[200,128]{1,0:T(8,128)S(1)}, u32[]{:S(2)}, u32[]{:S(2)}) %collective-permute-start.8) | collective-permute-done | bytes 102432 | tf_op jit(solution)/shard_map/ppermute | solution.py:400
  37.2 2.8 %collective-permute-done.7 = f32[200,128]{1,0:T(8,128)S(1)} collective-permute-done((f32[200,128]{1,0:T(8,128)S(1)}, f32[200,128]{1,0:T(8,128)S(1)}, u32[]{:S(2)}, u32[]{:S(2)}) %collective-permute-start.7) | collective-permute-done | bytes 102432 | tf_op jit(solution)/shard_map/ppermute | solution.py:400
  40.0 0.0 collective-permute-done.6
  40.0 0.1 collective-permute-start.9
  40.1 1.3 %collective-permute-done.9.theirs = f32[200,128]{1,0:T(8,128)S(1)} collective-permute-done((f32[200,128]{1,0:T(8,128)S(1)}, f32[200,128]{1,0:T(8,128)S(1)}, u32[]{:S(2)}, u32[]{:S(2)}) %collective-permute-start.9) | collective-permute-done | bytes 102432 | tf_op jit(solution)/shard_map/ppermute | solution.py:404
  41.4 0.0 copy-done.2
  41.4 7.3 %finish.1 = (f32[1024,128]{1,0:T(8,128)}, f32[1024,128]{1,0:T(8,128)}, f32[1024,128]{1,0:T(8,128)}) custom-call(s32[4]{0:T(128)S(1)} %pad_add_fusion.scalars, s32[1,128]{1,0:T(1,128)S(1)} %copy-done.2, f32[200,128]{1,0:T(8,128)S(1)} %add_add_fusion.mine, f32[200,128]{1,0:T(8,128)S(1)} %collective-permute-done.9.theirs, bf16[1040,128]{1,0:T(8,128)(2,1)S(1)} %round.1.packed, ...), custom_call_target="tpu_custom_call" | custom-call | tf_op jit(solution)/shard_map/finish/pallas_call | solution.py:405
  (3 shorter events, 0.1 us)
Async XLA Ops:
  0.6 13.1 %copy-start.1 = (s32[1,1024]{1,0:T(1,128)S(1)}, s32[1,1024]{1,0:T(1,128)}, u32[]{:S(2)}) copy-start(s32[1,1024]{1,0:T(1,128)} %param.8) | copy-start | bytes 12292
  2.5 9.4 %collective-permute-start = (bf16[1040,128]{1,0:T(8,128)(2,1)S(1)}, bf16[1040,128]{1,0:T(8,128)(2,1)S(1)}, u32[]{:S(2)}, u32[]{:S(2)}) collective-permute-start(bf16[1040,128]{1,0:T(8,128)(2,1)S(1)} %round.1.packed), channel_id=1, source_target_pairs={{0,4},{4,0},{8,12},{12,8},{16,20},{20,16},{24,28},{28,24},{1,5},{5... | collective-permute-start | bytes 798728 | tf_op jit(solution)/shard_map/ppermute | solution.py:354
  5.6 13.9 %copy-start = (f32[1,1024,128]{2,1,0:T(8,128)S(1)}, f32[1,1024,128]{2,1,0:T(8,128)}, u32[]{:S(2)}) copy-start(f32[1,1024,128]{2,1,0:T(8,128)} %param.6) | copy-start | bytes 1572868
  8.7 32.7 %copy-start.2 = (s32[1,128]{1,0:T(1,128)S(1)}, s32[1,128]{1,0:T(1,128)}, u32[]{:S(2)}) copy-start(s32[1,128]{1,0:T(1,128)} %kept.3) | copy-start | bytes 1540
  11.9 7.6 %collective-permute-start.1 = (bf16[1040,128]{1,0:T(8,128)(2,1)S(1)}, bf16[1040,128]{1,0:T(8,128)(2,1)S(1)}, u32[]{:S(2)}, u32[]{:S(2)}) collective-permute-start(bf16[1040,128]{1,0:T(8,128)(2,1)S(1)} %collective-permute-done.other), channel_id=1, source_target_pairs={{0,8},{8,16},{16,24},{24,28},{4,0},{12,4},{20,12},{28,20},{1,9},{9... | collective-permute-start | bytes 798728 | tf_op jit(solution)/shard_map/ppermute | solution.py:369
  21.6 1.4 %collective-permute-start.2 = (f32[200,128]{1,0:T(8,128)S(1)}, f32[200,128]{1,0:T(8,128)S(1)}, u32[]{:S(2)}, u32[]{:S(2)}) collective-permute-start(f32[200,128]{1,0:T(8,128)S(1)} %get-tuple-element.15), channel_id=1, source_target_pairs={{0,1},{1,0},{2,3},{3,2},{4,5},{5,4},{6,7},{7,6},{8,9},{9,8},{10,11... | collective-permute-start | bytes 307208 | tf_op jit(solution)/shard_map/ppermute | solution.py:398
  23.0 5.6 %collective-permute-start.5 = (f32[200,128]{1,0:T(8,128)S(1)}, f32[200,128]{1,0:T(8,128)S(1)}, u32[]{:S(2)}, u32[]{:S(2)}) collective-permute-start(f32[200,128]{1,0:T(8,128)S(1)} %add.26), channel_id=1, source_target_pairs={{0,6},{1,25},{2,4},{3,27},{4,2},{5,29},{6,0},{7,31},{8,14},{9,17},... | collective-permute-start | bytes 307208 | tf_op jit(solution)/shard_map/ppermute | solution.py:400
  25.2 4.7 %collective-permute-start.4 = (f32[200,128]{1,0:T(8,128)S(1)}, f32[200,128]{1,0:T(8,128)S(1)}, u32[]{:S(2)}, u32[]{:S(2)}) collective-permute-start(f32[200,128]{1,0:T(8,128)S(1)} %add.26), channel_id=1, source_target_pairs={{0,4},{1,17},{2,6},{3,19},{4,0},{5,21},{6,2},{7,23},{8,12},{9,25},... | collective-permute-start | bytes 307208 | tf_op jit(solution)/shard_map/ppermute | solution.py:400
  25.9 4.7 %collective-permute-start.3 = (f32[200,128]{1,0:T(8,128)S(1)}, f32[200,128]{1,0:T(8,128)S(1)}, u32[]{:S(2)}, u32[]{:S(2)}) collective-permute-start(f32[200,128]{1,0:T(8,128)S(1)} %add.26), channel_id=1, source_target_pairs={{0,2},{1,9},{2,0},{3,11},{4,6},{5,13},{6,4},{7,15},{8,10},{9,1},{1... | collective-permute-start | bytes 307208 | tf_op jit(solution)/shard_map/ppermute | solution.py:400
  30.6 6.6 %collective-permute-start.8 = (f32[200,128]{1,0:T(8,128)S(1)}, f32[200,128]{1,0:T(8,128)S(1)}, u32[]{:S(2)}, u32[]{:S(2)}) collective-permute-start(f32[200,128]{1,0:T(8,128)S(1)} %add_add_fusion.1), channel_id=1, source_target_pairs={{0,24},{1,7},{2,26},{3,5},{4,28},{5,3},{6,30},{7,1},{8,16},{9,15},... | collective-permute-start | bytes 307208 | tf_op jit(solution)/shard_map/ppermute | solution.py:400
  34.2 5.8 %collective-permute-start.7 = (f32[200,128]{1,0:T(8,128)S(1)}, f32[200,128]{1,0:T(8,128)S(1)}, u32[]{:S(2)}, u32[]{:S(2)}) collective-permute-start(f32[200,128]{1,0:T(8,128)S(1)} %add_add_fusion.1), channel_id=1, source_target_pairs={{0,16},{1,5},{2,18},{3,7},{4,20},{5,1},{6,22},{7,3},{8,24},{9,13},... | collective-permute-start | bytes 307208 | tf_op jit(solution)/shard_map/ppermute | solution.py:400
  34.2 5.8 %collective-permute-start.6 = (f32[200,128]{1,0:T(8,128)S(1)}, f32[200,128]{1,0:T(8,128)S(1)}, u32[]{:S(2)}, u32[]{:S(2)}) collective-permute-start(f32[200,128]{1,0:T(8,128)S(1)} %add_add_fusion.1), channel_id=1, source_target_pairs={{0,8},{1,3},{2,10},{3,1},{4,12},{5,7},{6,14},{7,5},{8,0},{9,11},{1... | collective-permute-start | bytes 307208 | tf_op jit(solution)/shard_map/ppermute | solution.py:400
  40.0 1.4 %collective-permute-start.9 = (f32[200,128]{1,0:T(8,128)S(1)}, f32[200,128]{1,0:T(8,128)S(1)}, u32[]{:S(2)}, u32[]{:S(2)}) collective-permute-start(f32[200,128]{1,0:T(8,128)S(1)} %add_add_fusion.mine), channel_id=1, source_target_pairs={{0,1},{1,0},{2,3},{3,2},{4,5},{5,4},{6,7},{7,6},{8,9},{9,8},{10,11... | collective-permute-start | bytes 307208 | tf_op jit(solution)/shard_map/ppermute | solution.py:404

commit v2 on v1

--- a/solution.py
+++ b/solution.py
@@ -14,6 +14,7 @@
 AXES = ("clu", "sub")
 VMEM_BYTES = 24 * 2**20
 COPIES = 4
+PIECES = 1
 SMEM = pl.BlockSpec(memory_space=pltpu.SMEM)
 VMEM = pl.BlockSpec(memory_space=pltpu.VMEM)
 HBM = pl.BlockSpec(memory_space=pltpu.HBM)
@@ -28,6 +29,14 @@
     return jnp.dot(a, b, preferred_element_type=f32, precision=lax.Precision.HIGHEST)
 
 
+def nearly(a, b):
+    columns = b.shape[1]
+    a_high, a_low = two_parts(a)
+    b_high, b_low = two_parts(b)
+    first = dot(a_high, jnp.concatenate([b_high, b_low], 1))
+    return first[:, :columns] + first[:, columns:] + dot(a_low, b_high)
+
+
 def gram(a, b):
     return lax.dot_general(a, b, (((0,), (0,)), ((), ())), preferred_element_type=f32)
 
@@ -49,7 +58,8 @@
     return start + lax.broadcasted_iota(jnp.int32, (rows, columns), 0) < scalars[SIZE]
 
 
-def round_kernel(sizes, rhs, kept, pairing, out, block, flags, rows, done):
+def round_kernel(sizes, rhs, kept, pairing, *refs):
+    outs, (listed, block, flags, rows, done) = refs[:PIECES], refs[PIECES:]
     copies = [
         pltpu.make_async_copy(source, target, done.at[i])
         for i, (source, target) in enumerate(
@@ -63,19 +73,14 @@
     height, breadth = block.shape
     live = lax.broadcasted_iota(jnp.int32, (height, breadth), 0) < sizes[0]
     keep = flags[...].astype(f32)
-    out[0:height, :] = (jnp.where(live, block[...], 0.0) * keep).astype(bf16)
+    rounded = (jnp.where(live, block[...], 0.0) * keep).astype(bf16)
+    step = height // PIECES
+    for i, out in enumerate(outs):
+        out[0:step, :] = rounded[i * step : (i + 1) * step]
     order = rows[...]
+    listed[...] = order.astype(f32)
     digits = jnp.concatenate([order // 256, order % 256], 0)
-    out[height:, :] = digits.astype(f32).astype(bf16)
-
-
-def local_kernel(scalars, operator, packed, out):
-    rows, height = operator.shape
-    place = scalars[PLACE]
-    degree = (place > 0).astype(f32) + (place < scalars[LAST]).astype(f32)
-    here = pl.ds(pl.multiple_of(pl.program_id(0) * rows, rows), rows)
-    own = packed[here, :].astype(f32)
-    out[here, :] = dot(operator[...], packed[0:height, :]) + (stiffness * degree) * own
+    outs[-1][step:, :] = digits.astype(f32).astype(bf16)
 
 
 def picked(block, pairing, start, rows, inverse):
@@ -104,23 +109,47 @@
     return dot(chosen, block)
 
 
-def sent_pairing(packed, height):
-    digits = packed[height:, :].astype(f32)
+def joined(pieces, height):
+    step = height // PIECES
+    return jnp.concatenate([piece[0:step, :] for piece in pieces], 0)
+
+
+def sent_pairing(pieces, height):
+    digits = pieces[-1][height // PIECES :, :].astype(f32)
     half = digits.shape[0] // 2
     return digits[:half] * 256.0 + digits[half:]
 
 
-def near_kernel(scalars, pairing, other, base, out):
-    height = base.shape[0]
+def local_kernel(scalars, operator, *refs):
+    own, (out, matrix, done) = refs[:PIECES], refs[PIECES:]
+    height = out.shape[0]
+    step = min(height, 256)
+    strips = [slice(start, start + step) for start in range(0, height, step)]
+    copies = [
+        pltpu.make_async_copy(operator.at[rows], matrix.at[rows], done.at[i])
+        for i, rows in enumerate(strips)
+    ]
+    for copy in copies:
+        copy.start()
+    place = scalars[PLACE]
+    degree = (place > 0).astype(f32) + (place < scalars[LAST]).astype(f32)
+    block = joined(own, height)
+    for rows, copy in zip(strips, copies):
+        copy.wait()
+        out[rows, :] = dot(matrix[rows, :], block) + (stiffness * degree) * block[rows].astype(f32)
+
+
+def near_kernel(scalars, pairing, base, *refs):
+    other, out = refs[:PIECES], refs[PIECES]
+    height = out.shape[0]
     step = min(height, 256)
     even = scalars[PLACE] % 2 == 0
 
     def go(rows_of, inverse):
+        block = joined(other, height)
         for start in range(0, height, step):
             rows = slice(start, start + step)
-            out[rows, :] = base[rows, :] - stiffness * picked(
-                other[0:height, :], rows_of, start, step, inverse
-            )
+            out[rows, :] = base[rows, :] - stiffness * picked(block, rows_of, start, step, inverse)
 
     @pl.when(even)
     def _():
@@ -128,10 +157,12 @@
 
     @pl.when(jnp.logical_not(even))
     def _():
-        go(pairing[...].astype(f32), False)
-
-
-def sums_kernel(scalars, pairing, other, base, packed, rhs, upper, lower, mine, theirs, image, stack):
+        go(pairing[...], False)
+
+
+def sums_kernel(scalars, pairing, base, rhs, *refs):
+    other, own = refs[:PIECES], refs[PIECES : 2 * PIECES]
+    upper, lower, mine, theirs, image, stack = refs[2 * PIECES :]
     height, breadth = base.shape
     step = min(height, 256)
     place = scalars[PLACE]
@@ -140,16 +171,15 @@
     within = jnp.where(outer, 0.0, stiffness)
 
     def go(rows_of, inverse):
+        block = joined(other, height)
         for start in range(0, height, step):
             rows = slice(start, start + step)
-            whole = base[rows, :] - within * picked(
-                other[0:height, :], rows_of, start, step, inverse
-            )
+            whole = base[rows, :] - within * picked(block, rows_of, start, step, inverse)
             image[rows, :] = jnp.where(live_rows(scalars, start, step, breadth), whole, 0.0)
 
     @pl.when(even)
     def _():
-        go(pairing[...].astype(f32), False)
+        go(pairing[...], False)
 
     @pl.when(jnp.logical_not(even))
     def _():
@@ -161,7 +191,7 @@
     residual = jnp.where(live_rows(scalars, 0, height, breadth), rhs[...], 0.0)
     res_high, res_low = two_parts(residual)
     right = jnp.concatenate([high, low, res_high, res_low], 1)
-    first = gram(packed[0:height, :], right)
+    first = gram(joined(own, height), right)
     second = gram(high, right)
     third = gram(low, res_high)
     b = breadth
@@ -192,12 +222,13 @@
     scaled = regular * scale_row * scale_column
     error = one - scaled
 
-    def factor(guess, now):
-        both = exact(jnp.concatenate([guess, now], 0), now)
+    def factor(guess, now, product):
+        both = product(jnp.concatenate([guess, now], 0), now)
         return guess + both[:size], both[size:]
 
-    guess, now = factor(*factor(one + error, exact(error, error)))
-    total[...] = guess + exact(guess, now)
+    guess, now = factor(one + error, nearly(error, error), nearly)
+    guess, now = factor(guess, now, nearly)
+    total[...] = guess + nearly(guess, now)
 
     @pl.when(jnp.logical_not(jnp.sum(now * now) < 1e-6))
     def _():
@@ -212,7 +243,7 @@
             return jnp.logical_and(norm > 1e-6, count < 48)
 
         def again(state):
-            guess, now = factor(total[...], power[...])
+            guess, now = factor(total[...], power[...], exact)
             total[...] = guess
             power[...] = now
             return state[0] + 1, jnp.sum(now * now)
@@ -225,9 +256,10 @@
 
 
 def finish_kernel(
-    scalars, kept, mine, theirs, packed, upper, lower, rhs, solution, residual, direction,
-    stack, total, power, results, done,
+    scalars, kept, mine, theirs, upper, lower, rhs, *refs
 ):
+    own, (solution, residual, direction) = refs[:PIECES], refs[PIECES : PIECES + 3]
+    stack, total, power, results, done = refs[PIECES + 3 :]
     height, b = rhs.shape
     rows = results.shape[1] // COPIES
     half = mine.shape[0]
@@ -250,6 +282,7 @@
     correction = exact(inverse, coupled)
     weight_parts = jnp.concatenate(two_parts(weights), 1)
     correction_parts = jnp.concatenate(two_parts(correction), 1)
+    packed = joined(own, height)
     copies = []
 
     def send(which, target, piece):
@@ -260,7 +293,7 @@
 
     for piece in range(COPIES):
         part = slice(piece * rows, (piece + 1) * rows)
-        product = dot(packed[part, :], weight_parts)
+        product = dot(packed[part], weight_parts)
         results[0, part, :] = product[:, :b] + product[:, b:]
         send(0, solution, piece)
         moved = dot(upper[part, :], weight_parts)
@@ -270,7 +303,7 @@
         send(1, residual, piece)
     for piece in range(COPIES):
         part = slice(piece * rows, (piece + 1) * rows)
-        product = dot(packed[part, :], correction_parts)
+        product = dot(packed[part], correction_parts)
         results[2, part, :] = results[1, part, :] - (product[:, :b] + product[:, b:])
         send(2, direction, piece)
     for copy in copies:
@@ -337,11 +370,13 @@
     cost = pl.CostEstimate(
         flops=2 * height * height * breadth, bytes_accessed=2 * height * height, transcendentals=0
     )
-    packed = pl.pallas_call(
+    piece = height // PIECES
+    shapes = [like((piece, breadth), bf16)] * (PIECES - 1) + [like((piece + extra, breadth), bf16)]
+    *packed, listed = pl.pallas_call(
         round_kernel,
-        out_shape=like((height + extra, breadth), bf16),
+        out_shape=(*shapes, like(pairing.shape, f32)),
         in_specs=[SMEM] + [HBM] * 3,
-        out_specs=VMEM,
+        out_specs=(VMEM,) * (PIECES + 1),
         scratch_shapes=[
             pltpu.VMEM((height, breadth), f32),
             pltpu.VMEM((1, breadth), jnp.int32),
@@ -351,31 +386,32 @@
         compiler_params=parameters(),
         name="round",
     )(interface_sizes, *map(in_hbm, (right_side, kept_columns, pairing)))
-    other = lax.ppermute(packed, "clu", [(i, i ^ 1) for i in range(clusters) if i ^ 1 < clusters])
-    tile = min(height, 256)
+    pairs = [(i, i ^ 1) for i in range(clusters)]
+    other = [lax.ppermute(part, "clu", pairs) for part in packed]
+    strips = height // min(height, 256)
     base = pl.pallas_call(
         local_kernel,
-        grid=(height // tile,),
         out_shape=like((height, breadth), f32),
-        in_specs=[SMEM, pl.BlockSpec((tile, height), lambda i: (i, 0)), VMEM],
+        in_specs=[SMEM, HBM] + [VMEM] * PIECES,
         out_specs=VMEM,
+        scratch_shapes=[pltpu.VMEM((height, height), bf16), pltpu.SemaphoreType.DMA((strips,))],
         compiler_params=parameters(),
         cost_estimate=cost,
         name="local",
-    )(scalars, in_hbm(matrix), packed)
-    other, base = lax.optimization_barrier((other, base))
+    )(scalars, in_hbm(matrix), *packed)
+    other[0], base = lax.optimization_barrier((other[0], base))
     onward = [(i, i + 2 if i + 2 < clusters else i + 1) for i in range(0, clusters, 2)]
     onward += [(i, max(i - 2, 0)) for i in range(1, clusters, 2)]
-    outside = lax.ppermute(other, "clu", onward)
+    outside = [lax.ppermute(part, "clu", onward) for part in other]
     nearer = pl.pallas_call(
         near_kernel,
         out_shape=like((height, breadth), f32),
-        in_specs=[SMEM] + [VMEM] * 3,
+        in_specs=[SMEM] + [VMEM] * (2 + PIECES),
         out_specs=VMEM,
         compiler_params=parameters(),
         cost_estimate=cost,
         name="near",
-    )(scalars, pairing, other, base)
+    )(scalars, listed, base, *other)
     half = (3 * breadth + 16) // 2
     upper, lower, mine, theirs = pl.pallas_call(
         sums_kernel,
@@ -385,7 +421,7 @@
             like((half, breadth), f32),
             like((half, breadth), f32),
         ),
-        in_specs=[SMEM] + [VMEM] * 5,
+        in_specs=[SMEM] + [VMEM] * (3 + 2 * PIECES),
         out_specs=(VMEM,) * 4,
         scratch_shapes=[
             pltpu.VMEM((height, breadth), f32),
@@ -393,7 +429,7 @@
         ],
         compiler_params=parameters(),
         name="sums",
-    )(scalars, pairing, outside, nearer, packed, right_side)
+    )(scalars, listed, nearer, right_side, *outside, *packed)
     swap = [(i, i ^ 1) for i in range(clusters * places)]
     mine = mine + lax.ppermute(theirs, AXES, swap)
     for routes in rounds_of(clusters, places):
@@ -405,7 +441,7 @@
     outs = pl.pallas_call(
         finish_kernel,
         out_shape=(like((height, breadth), f32),) * 3,
-        in_specs=[SMEM] + [VMEM] * 7,
+        in_specs=[SMEM] + [VMEM] * (6 + PIECES),
         out_specs=(HBM,) * 3,
         scratch_shapes=[
             pltpu.VMEM((2 * half, breadth), f32),
@@ -416,7 +452,7 @@
         ],
         compiler_params=parameters(),
         name="finish",
-    )(scalars, kept_columns, mine, theirs, packed, upper, lower, right_side)
+    )(scalars, kept_columns, mine, theirs, upper, lower, right_side, *packed)
     return tuple(out[None] for out in outs)
 
 

time: 49 us -> 48.4 us (0.988)
  Pallas kernels: 14.9 us -> 13.9 us
    pallas_call x1, Pallas kernels: 7.35 us -> 6.62 us  [per_device(): pl.pallas_call(finish_kernel, out_shape=(like((height, breadth), f32),) *...]
  transfers between devices with their start and end apart: 10 -> 10, of which waited for: 9 -> 9; matrix products, arithmetic and copies ran while one was open for 0% -> 0% of each run, Pallas kernels for 9% -> 8%
where the time goes in v2:
time: 48.4 us; the launch traced here: 48 us
  waiting for transfers between devices  19.7 us (41%)
  Pallas kernels  13.9 us (29%)
  starting transfers between devices  13 us (27%)
  between operations  1.34 us (3%)
    ppermute x6, waiting for transfers between devices, per_device(): parts = [mine] + [lax.ppermute(mine, AXES, route) for route in routes]  9 us
    ppermute x6, starting transfers between devices, per_device(): parts = [mine] + [lax.ppermute(mine, AXES, route) for route in routes]  8.01 us
    pallas_call x1, Pallas kernels, per_device(): pl.pallas_call(finish_kernel, out_shape=(like((height, breadth), f32),) *...  6.62 us
    ppermute x1, waiting for transfers between devices, per_device(): outside = [lax.ppermute(part, 'clu', onward) for part in other]  4.51 us
    ppermute x1, waiting for transfers between devices, per_device(): other = [lax.ppermute(part, 'clu', pairs) for part in packed]  3.55 us
    ppermute x1, starting transfers between devices, per_device(): other = [lax.ppermute(part, 'clu', pairs) for part in packed]  3.03 us
    pallas_call x1, Pallas kernels, per_device(): pl.pallas_call(local_kernel, out_shape=like((height, breadth), f32), in_s...  2.76 us
    pallas_call x1, Pallas kernels, per_device(): pl.pallas_call(sums_kernel, out_shape=(like((height, breadth), bf16), lik...  2.08 us
  transfers between devices with their start and end apart: 10, of which 9 were waited for; matrix products, arithmetic and copies ran while one was open for 0% of the time, Pallas kernels for 8%

profile of v2, /device:TPU:0, one launch (start us, length us, event | category | flops | bytes accessed | tf_op | source)
XLA Modules:
  0.0 48.0 jit_solution(3655567100891911534)
XLA Ops:
  1.3 1.2 %round.1 = (bf16[1040,128]{1,0:T(8,128)(2,1)S(1)}, f32[8,128]{1,0:T(8,128)S(1)}) custom-call(s32[1]{0:T(128)S(6)} %copy.8.sizes, f32[1024,128]{1,0:T(8,128)} %bitcast.8, s32[1,128]{1,0:T(1,128)} %kept.3, s32[8,128]{1,0:T(8,128)} %bitcast.12), custom_call_target="tpu_custom_call" | custom-call | tf_op jit(solution)/shard_map/round/pallas_call | solution.py:375
  2.4 3.0 %collective-permute-start = (bf16[1040,128]{1,0:T(8,128)(2,1)S(1)}, bf16[1040,128]{1,0:T(8,128)(2,1)S(1)}, u32[]{:S(2)}, u32[]{:S(2)}) collective-permute-start(bf16[1040,128]{1,0:T(8,128)(2,1)S(1)} %get-tuple-element.15.refs_0_.refs_1_), channel_id=1, source_target_pairs={{0,4},{4,0},{8,12},{12,8},{16,20},{20,16},{24,28},{28,24},{1,5},{5... | collective-permute-start | bytes 798728 | tf_op jit(solution)/shard_map/ppermute | solution.py:390
  5.5 0.1 pad_add_fusion.scalars
  5.6 0.0 copy-start
  5.6 2.8 %local.1.base = f32[1024,128]{1,0:T(8,128)S(1)} custom-call(s32[4]{0:T(128)S(1)} %pad_add_fusion.scalars, bf16[1024,1024]{1,0:T(8,128)(2,1)} %bitcast.11, bf16[1040,128]{1,0:T(8,128)(2,1)S(1)} %get-tuple-element.15.refs_0_.refs_1_), custom_call_target="tpu_custom_call" | custom-call | flops 268435456 | bytes 2097152 | tf_op jit(solution)/shard_map/local/pallas_call | solution.py:392
  8.3 3.5 %collective-permute-done.refs_0_ = bf16[1040,128]{1,0:T(8,128)(2,1)S(1)} collective-permute-done((bf16[1040,128]{1,0:T(8,128)(2,1)S(1)}, bf16[1040,128]{1,0:T(8,128)(2,1)S(1)}, u32[]{:S(2)}, u32[]{:S(2)}) %collective-permute-start) | collective-permute-done | bytes 266272 | tf_op jit(solution)/shard_map/ppermute | solution.py:390
  11.9 1.8 %collective-permute-start.1 = (bf16[1040,128]{1,0:T(8,128)(2,1)S(1)}, bf16[1040,128]{1,0:T(8,128)(2,1)S(1)}, u32[]{:S(2)}, u32[]{:S(2)}) collective-permute-start(bf16[1040,128]{1,0:T(8,128)(2,1)S(1)} %collective-permute-done.refs_0_), channel_id=1, source_target_pairs={{0,8},{8,16},{16,24},{24,28},{4,0},{12,4},{20,12},{28,20},{1,9},{9... | collective-permute-start | bytes 798728 | tf_op jit(solution)/shard_map/ppermute | solution.py:405
  13.7 0.0 copy-start.1
  13.7 1.3 %near.1.base = f32[1024,128]{1,0:T(8,128)S(1)} custom-call(s32[4]{0:T(128)S(1)} %pad_add_fusion.scalars, f32[8,128]{1,0:T(8,128)S(1)} %get-tuple-element.14.pairing, f32[1024,128]{1,0:T(8,128)S(1)} %local.1.base, bf16[1040,128]{1,0:T(8,128)(2,1)S(1)} %collective-permute-done.refs_0_), custom_call_target="tpu_custom_call" | custom-call | flops 268435456 | bytes 2097152 | tf_op jit(solution)/shard_map/near/pallas_call | solution.py:406
  14.9 4.5 %collective-permute-done.1.refs_0_ = bf16[1040,128]{1,0:T(8,128)(2,1)S(1)} collective-permute-done((bf16[1040,128]{1,0:T(8,128)(2,1)S(1)}, bf16[1040,128]{1,0:T(8,128)(2,1)S(1)}, u32[]{:S(2)}, u32[]{:S(2)}) %collective-permute-start.1) | collective-permute-done | bytes 266272 | tf_op jit(solution)/shard_map/ppermute | solution.py:405
  19.5 0.0 copy-done
  19.5 2.1 %sums.1 = (bf16[1024,128]{1,0:T(8,128)(2,1)S(1)}, bf16[1024,128]{1,0:T(8,128)(2,1)S(1)}, f32[200,128]{1,0:T(8,128)S(1)}, f32[200,128]{1,0:T(8,128)S(1)}) custom-call(s32[4]{0:T(128)S(1)} %pad_add_fusion.scalars, f32[8,128]{1,0:T(8,128)S(1)} %get-tuple-element.14.pairing, f32[1024,128]{1,0:T(8,128)S(1)} %near.1.base, f32[1024,128]{1,0:T(8,128)S(1)} %bitcast.9, ...), custom_call_target="tpu_custom_call" | custom-call | tf_op jit(solution)/shard_map/sums/pallas_call | solution.py:416
  21.5 0.1 collective-permute-start.2
  21.6 1.3 %collective-permute-done.2 = f32[200,128]{1,0:T(8,128)S(1)} collective-permute-done((f32[200,128]{1,0:T(8,128)S(1)}, f32[200,128]{1,0:T(8,128)S(1)}, u32[]{:S(2)}, u32[]{:S(2)}) %collective-permute-start.2) | collective-permute-done | bytes 102432 | tf_op jit(solution)/shard_map/ppermute | solution.py:434
  22.9 2.2 %collective-permute-start.5 = (f32[200,128]{1,0:T(8,128)S(1)}, f32[200,128]{1,0:T(8,128)S(1)}, u32[]{:S(2)}, u32[]{:S(2)}) collective-permute-start(f32[200,128]{1,0:T(8,128)S(1)} %add.26), channel_id=1, source_target_pairs={{0,6},{1,25},{2,4},{3,27},{4,2},{5,29},{6,0},{7,31},{8,14},{9,17},... | collective-permute-start | bytes 307208 | tf_op jit(solution)/shard_map/ppermute | solution.py:436
  25.1 0.7 %collective-permute-start.4 = (f32[200,128]{1,0:T(8,128)S(1)}, f32[200,128]{1,0:T(8,128)S(1)}, u32[]{:S(2)}, u32[]{:S(2)}) collective-permute-start(f32[200,128]{1,0:T(8,128)S(1)} %add.26), channel_id=1, source_target_pairs={{0,4},{1,17},{2,6},{3,19},{4,0},{5,21},{6,2},{7,23},{8,12},{9,25},... | collective-permute-start | bytes 307208 | tf_op jit(solution)/shard_map/ppermute | solution.py:436
  25.9 0.6 %collective-permute-start.3 = (f32[200,128]{1,0:T(8,128)S(1)}, f32[200,128]{1,0:T(8,128)S(1)}, u32[]{:S(2)}, u32[]{:S(2)}) collective-permute-start(f32[200,128]{1,0:T(8,128)S(1)} %add.26), channel_id=1, source_target_pairs={{0,2},{1,9},{2,0},{3,11},{4,6},{5,13},{6,4},{7,15},{8,10},{9,1},{1... | collective-permute-start | bytes 307208 | tf_op jit(solution)/shard_map/ppermute | solution.py:436
  26.5 2.1 %collective-permute-done.5 = f32[200,128]{1,0:T(8,128)S(1)} collective-permute-done((f32[200,128]{1,0:T(8,128)S(1)}, f32[200,128]{1,0:T(8,128)S(1)}, u32[]{:S(2)}, u32[]{:S(2)}) %collective-permute-start.5) | collective-permute-done | bytes 102432 | tf_op jit(solution)/shard_map/ppermute | solution.py:436
  28.6 1.3 %collective-permute-done.4 = f32[200,128]{1,0:T(8,128)S(1)} collective-permute-done((f32[200,128]{1,0:T(8,128)S(1)}, f32[200,128]{1,0:T(8,128)S(1)}, u32[]{:S(2)}, u32[]{:S(2)}) %collective-permute-start.4) | collective-permute-done | bytes 102432 | tf_op jit(solution)/shard_map/ppermute | solution.py:436
  29.8 0.7 %collective-permute-done.3 = f32[200,128]{1,0:T(8,128)S(1)} collective-permute-done((f32[200,128]{1,0:T(8,128)S(1)}, f32[200,128]{1,0:T(8,128)S(1)}, u32[]{:S(2)}, u32[]{:S(2)}) %collective-permute-start.3) | collective-permute-done | bytes 102432 | tf_op jit(solution)/shard_map/ppermute | solution.py:436
  30.5 3.7 %collective-permute-start.8 = (f32[200,128]{1,0:T(8,128)S(1)}, f32[200,128]{1,0:T(8,128)S(1)}, u32[]{:S(2)}, u32[]{:S(2)}) collective-permute-start(f32[200,128]{1,0:T(8,128)S(1)} %add_add_fusion.1), channel_id=1, source_target_pairs={{0,24},{1,7},{2,26},{3,5},{4,28},{5,3},{6,30},{7,1},{8,16},{9,15},... | collective-permute-start | bytes 307208 | tf_op jit(solution)/shard_map/ppermute | solution.py:436
  34.2 0.0 collective-permute-start.7
  34.2 0.8 %collective-permute-start.6 = (f32[200,128]{1,0:T(8,128)S(1)}, f32[200,128]{1,0:T(8,128)S(1)}, u32[]{:S(2)}, u32[]{:S(2)}) collective-permute-start(f32[200,128]{1,0:T(8,128)S(1)} %add_add_fusion.1), channel_id=1, source_target_pairs={{0,8},{1,3},{2,10},{3,1},{4,12},{5,7},{6,14},{7,5},{8,0},{9,11},{1... | collective-permute-start | bytes 307208 | tf_op jit(solution)/shard_map/ppermute | solution.py:436
  35.0 2.2 %collective-permute-done.8 = f32[200,128]{1,0:T(8,128)S(1)} collective-permute-done((f32[200,128]{1,0:T(8,128)S(1)}, f32[200,128]{1,0:T(8,128)S(1)}, u32[]{:S(2)}, u32[]{:S(2)}) %collective-permute-start.8) | collective-permute-done | bytes 102432 | tf_op jit(solution)/shard_map/ppermute | solution.py:436
  37.2 2.8 %collective-permute-done.7 = f32[200,128]{1,0:T(8,128)S(1)} collective-permute-done((f32[200,128]{1,0:T(8,128)S(1)}, f32[200,128]{1,0:T(8,128)S(1)}, u32[]{:S(2)}, u32[]{:S(2)}) %collective-permute-start.7) | collective-permute-done | bytes 102432 | tf_op jit(solution)/shard_map/ppermute | solution.py:436
  40.0 0.0 collective-permute-done.6
  40.0 0.1 collective-permute-start.9
  40.1 1.3 %collective-permute-done.9.theirs = f32[200,128]{1,0:T(8,128)S(1)} collective-permute-done((f32[200,128]{1,0:T(8,128)S(1)}, f32[200,128]{1,0:T(8,128)S(1)}, u32[]{:S(2)}, u32[]{:S(2)}) %collective-permute-start.9) | collective-permute-done | bytes 102432 | tf_op jit(solution)/shard_map/ppermute | solution.py:440
  41.4 0.0 copy-done.1
  41.4 6.6 %finish.1 = (f32[1024,128]{1,0:T(8,128)}, f32[1024,128]{1,0:T(8,128)}, f32[1024,128]{1,0:T(8,128)}) custom-call(s32[4]{0:T(128)S(1)} %pad_add_fusion.scalars, s32[1,128]{1,0:T(1,128)S(1)} %copy-done.1, f32[200,128]{1,0:T(8,128)S(1)} %add_add_fusion.mine, f32[200,128]{1,0:T(8,128)S(1)} %collective-permute-done.9.theirs, ...), custom_call_target="tpu_custom_call" | custom-call | tf_op jit(solution)/shard_map/finish/pallas_call | solution.py:441
  (3 shorter events, 0.1 us)
Async XLA Ops:
  2.4 9.4 %collective-permute-start = (bf16[1040,128]{1,0:T(8,128)(2,1)S(1)}, bf16[1040,128]{1,0:T(8,128)(2,1)S(1)}, u32[]{:S(2)}, u32[]{:S(2)}) collective-permute-start(bf16[1040,128]{1,0:T(8,128)(2,1)S(1)} %get-tuple-element.15.refs_0_.refs_1_), channel_id=1, source_target_pairs={{0,4},{4,0},{8,12},{12,8},{16,20},{20,16},{24,28},{28,24},{1,5},{5... | collective-permute-start | bytes 798728 | tf_op jit(solution)/shard_map/ppermute | solution.py:390
  5.6 13.9 %copy-start = (f32[1,1024,128]{2,1,0:T(8,128)S(1)}, f32[1,1024,128]{2,1,0:T(8,128)}, u32[]{:S(2)}) copy-start(f32[1,1024,128]{2,1,0:T(8,128)} %param.6) | copy-start | bytes 1572868
  11.9 7.6 %collective-permute-start.1 = (bf16[1040,128]{1,0:T(8,128)(2,1)S(1)}, bf16[1040,128]{1,0:T(8,128)(2,1)S(1)}, u32[]{:S(2)}, u32[]{:S(2)}) collective-permute-start(bf16[1040,128]{1,0:T(8,128)(2,1)S(1)} %collective-permute-done.refs_0_), channel_id=1, source_target_pairs={{0,8},{8,16},{16,24},{24,28},{4,0},{12,4},{20,12},{28,20},{1,9},{9... | collective-permute-start | bytes 798728 | tf_op jit(solution)/shard_map/ppermute | solution.py:405
  13.7 27.7 %copy-start.1 = (s32[1,128]{1,0:T(1,128)S(1)}, s32[1,128]{1,0:T(1,128)}, u32[]{:S(2)}) copy-start(s32[1,128]{1,0:T(1,128)} %kept.3) | copy-start | bytes 1540
  21.5 1.4 %collective-permute-start.2 = (f32[200,128]{1,0:T(8,128)S(1)}, f32[200,128]{1,0:T(8,128)S(1)}, u32[]{:S(2)}, u32[]{:S(2)}) collective-permute-start(f32[200,128]{1,0:T(8,128)S(1)} %get-tuple-element.19), channel_id=1, source_target_pairs={{0,1},{1,0},{2,3},{3,2},{4,5},{5,4},{6,7},{7,6},{8,9},{9,8},{10,11... | collective-permute-start | bytes 307208 | tf_op jit(solution)/shard_map/ppermute | solution.py:434
  22.9 5.6 %collective-permute-start.5 = (f32[200,128]{1,0:T(8,128)S(1)}, f32[200,128]{1,0:T(8,128)S(1)}, u32[]{:S(2)}, u32[]{:S(2)}) collective-permute-start(f32[200,128]{1,0:T(8,128)S(1)} %add.26), channel_id=1, source_target_pairs={{0,6},{1,25},{2,4},{3,27},{4,2},{5,29},{6,0},{7,31},{8,14},{9,17},... | collective-permute-start | bytes 307208 | tf_op jit(solution)/shard_map/ppermute | solution.py:436
  25.1 4.7 %collective-permute-start.4 = (f32[200,128]{1,0:T(8,128)S(1)}, f32[200,128]{1,0:T(8,128)S(1)}, u32[]{:S(2)}, u32[]{:S(2)}) collective-permute-start(f32[200,128]{1,0:T(8,128)S(1)} %add.26), channel_id=1, source_target_pairs={{0,4},{1,17},{2,6},{3,19},{4,0},{5,21},{6,2},{7,23},{8,12},{9,25},... | collective-permute-start | bytes 307208 | tf_op jit(solution)/shard_map/ppermute | solution.py:436
  25.9 4.7 %collective-permute-start.3 = (f32[200,128]{1,0:T(8,128)S(1)}, f32[200,128]{1,0:T(8,128)S(1)}, u32[]{:S(2)}, u32[]{:S(2)}) collective-permute-start(f32[200,128]{1,0:T(8,128)S(1)} %add.26), channel_id=1, source_target_pairs={{0,2},{1,9},{2,0},{3,11},{4,6},{5,13},{6,4},{7,15},{8,10},{9,1},{1... | collective-permute-start | bytes 307208 | tf_op jit(solution)/shard_map/ppermute | solution.py:436
  30.5 6.6 %collective-permute-start.8 = (f32[200,128]{1,0:T(8,128)S(1)}, f32[200,128]{1,0:T(8,128)S(1)}, u32[]{:S(2)}, u32[]{:S(2)}) collective-permute-start(f32[200,128]{1,0:T(8,128)S(1)} %add_add_fusion.1), channel_id=1, source_target_pairs={{0,24},{1,7},{2,26},{3,5},{4,28},{5,3},{6,30},{7,1},{8,16},{9,15},... | collective-permute-start | bytes 307208 | tf_op jit(solution)/shard_map/ppermute | solution.py:436
  34.2 5.8 %collective-permute-start.7 = (f32[200,128]{1,0:T(8,128)S(1)}, f32[200,128]{1,0:T(8,128)S(1)}, u32[]{:S(2)}, u32[]{:S(2)}) collective-permute-start(f32[200,128]{1,0:T(8,128)S(1)} %add_add_fusion.1), channel_id=1, source_target_pairs={{0,16},{1,5},{2,18},{3,7},{4,20},{5,1},{6,22},{7,3},{8,24},{9,13},... | collective-permute-start | bytes 307208 | tf_op jit(solution)/shard_map/ppermute | solution.py:436
  34.2 5.8 %collective-permute-start.6 = (f32[200,128]{1,0:T(8,128)S(1)}, f32[200,128]{1,0:T(8,128)S(1)}, u32[]{:S(2)}, u32[]{:S(2)}) collective-permute-start(f32[200,128]{1,0:T(8,128)S(1)} %add_add_fusion.1), channel_id=1, source_target_pairs={{0,8},{1,3},{2,10},{3,1},{4,12},{5,7},{6,14},{7,5},{8,0},{9,11},{1... | collective-permute-start | bytes 307208 | tf_op jit(solution)/shard_map/ppermute | solution.py:436
  40.0 1.4 %collective-permute-start.9 = (f32[200,128]{1,0:T(8,128)S(1)}, f32[200,128]{1,0:T(8,128)S(1)}, u32[]{:S(2)}, u32[]{:S(2)}) collective-permute-start(f32[200,128]{1,0:T(8,128)S(1)} %add_add_fusion.mine), channel_id=1, source_target_pairs={{0,1},{1,0},{2,3},{3,2},{4,5},{5,4},{6,7},{7,6},{8,9},{9,8},{10,11... | collective-permute-start | bytes 307208 | tf_op jit(solution)/shard_map/ppermute | solution.py:440
